TPU v7x, 512 devices: a whole 4x4x16 slice. The times are simulated.
512 devices in a mesh: dp: 64 (over z, x_hi, core), rep: 8 (over y, x_lo).
Axes of the slice: x: 4 (x_hi: 2, x_lo: 2; x = x_hi * 2 + x_lo), y: 4, z: 16, core: 2. Of those that a mesh axis runs over, the one named last changes fastest.
Arguments:
- grad_out: bfloat16 [49152, 2048], P('dp', 'rep'), may hold values from -16 to 16
- pre_act: bfloat16 [49152, 3072], P('dp', 'rep'), may hold values from -6 to 6
- up_weight: bfloat16 [3072, 2048], P('rep'), may hold values from -0.125 to 0.125
- down_weight: bfloat16 [2048, 3072], P(None, 'rep'), may hold values from -0.109375 to 0.109375
- slot_counts: int32 [64], P('dp'), may hold values from 384 to 768, as said below
Outputs:
- input_grad: bfloat16 [49152, 2048], P('dp')
- down_grad: float32 [2048, 3072], P('dp', 'rep')
Inputs may be any that keep to these rules, and one draw needn't show every extreme that they name: Row i * 768 + j is live exactly when j < slot_counts[i]; some index has all 768 slots live and some index exactly 384.
All inputs are finite; a program needn't handle non-finite values.
Results may differ from a plain program's by a relative error of at most 0.0049.
Values may be sent and summed in bfloat16 or wider, within the bound.
No kernel may reach another device: no remote copies, remote signals or barrier semaphores. Data moves between devices by JAX's collectives and lax.ppermute only.
A program may use at most 64 MiB of HBM per device.

v0:
```python
import jax
import jax.numpy as jnp
from jax import lax
from jax.sharding import Mesh
from jax.sharding import PartitionSpec as P

REP = ("rep_0", "rep_1")


def whole_of(array, axes, dim):
    if not axes:
        return array
    nearer = lax.all_gather(array, axes[-1], axis=dim, tiled=True)
    return whole_of(nearer, axes[:-1], dim)


def on_device(grad_out, pre_act, up_weight, down_weight, slot_counts):
    slot_rows = grad_out.shape[0]
    live_rows = (lax.iota(jnp.int32, slot_rows) < slot_counts[0])[:, None]
    grad_full = whole_of(grad_out, REP, 1)
    grad_live = jnp.where(live_rows, grad_full, jnp.zeros_like(grad_full))
    zero_pre = jnp.zeros_like(pre_act)
    hidden = jnp.where(live_rows, jnp.maximum(pre_act, zero_pre), zero_pre)
    data_ranks = lax.axis_size("dp")
    down_sum = lax.psum_scatter(
        lax.dot_general(
            grad_live, hidden, (((0,), (0,)), ((), ())), preferred_element_type=jnp.float32
        ),
        "dp",
        scatter_dimension=0,
        tiled=True,
    )
    down_grad = down_sum / data_ranks
    hidden_grad = jnp.dot(grad_live, down_weight, preferred_element_type=jnp.float32)
    pre_grad = jnp.where(pre_act > 0, hidden_grad, jnp.zeros_like(hidden_grad)).astype(jnp.bfloat16)
    partial_terms = jnp.dot(pre_grad, up_weight, preferred_element_type=jnp.float32)
    input_sum = lax.psum(partial_terms, REP)
    input_grad = input_sum.astype(jnp.bfloat16)
    return (input_grad, down_grad)


def solution(mesh):
    finer = Mesh(mesh.devices.reshape(mesh.shape["dp"], 4, 2), ("dp", "rep_0", "rep_1"))
    in_specs = (P("dp", REP), P("dp", REP), P(REP, None), P(None, REP), P("dp"))
    out_specs = (P("dp", None), P("dp", REP))
    return jax.shard_map(
        on_device, mesh=finer, in_specs=in_specs, out_specs=out_specs, check_vma=False
    )
```

profile of v0, /device:TPU:4, one launch (start us, length us, event | category | flops | bytes accessed | tf_op | source)
XLA Modules:
  0.0 350.7 jit_solution(8490427789314710554)
XLA Ops:
  7.2 0.0 copy-start
  7.2 0.0 all-gather.2.cloned.1.call-start
  7.2 13.1 %all_gather.6 = bf16[768,512]{1,0:T(8,128)(2,1)} all-gather(bf16[768,256]{1,0:T(8,128)(2,1)} %param.5), channel_id=1, replica_groups=mesh['dp'=64,'rep_0'=4,'rep_1'=2] {'rep_1'}, dimensions={1}, use_global_device_ids=true | all-gather | bytes 1179648 | tf_op jit(solution)/shard_map/all_gather | solution.py:13
  20.3 0.0 all-gather.2.cloned.1.call-update
  20.4 0.0 reduce-scatter.2.cloned.1.call-start
  21.1 51.1 %all-gather.2.cloned.1.call-done = bf16[768,2048]{1,0:T(8,128)(2,1)} async-done(((bf16[768,512]{1,0:T(8,128)(2,1)}), bf16[768,2048]{1,0:T(8,128)(2,1)}) %all-gather.2.cloned.1.call-update) | async-done | bytes 3145744 | tf_op jit(solution)/shard_map/all_gather | solution.py:13
  72.2 5.6 %fusion.1 = f32[2048,384]{1,0:T(8,128)} fusion(bf16[768,2048]{1,0:T(8,128)(2,1)} %all-gather.2.cloned.1.call-done, pred[768]{0:T(1024)(128)(4,1)S(1)} %iota_compare_fusion, bf16[768,384]{1,0:T(8,128)(2,1)} %param.6), kind=kOutput, calls=%fused_computation.3 | convolution fusion | flops 1210122240 | bytes 6882048 | tf_op jit(solution)/shard_map/dot_general | solution.py:26
  77.8 0.0 copy-start.1
  77.8 0.0 reduce-scatter.2.cloned.1.call-update
  77.9 0.0 copy-done
  77.9 1.4 copy-done.1
  79.2 8.1 %fusion.2 = f32[768,2048]{1,0:T(8,128)} fusion(bf16[384,2048]{1,0:T(8,128)(2,1)S(1)} %copy-done, bf16[2048,384]{1,0:T(8,128)(2,1)S(1)} %copy-done.1, bf16[768,2048]{1,0:T(8,128)(2,1)} %all-gather.2.cloned.1.call-done, pred[768]{0:T(1024)(128)(4,1)S(1)} %iota_compare_fusion, bf16[768,384]{1,0:T(8,128)(2,1)} %param.6), kind=kOutput, calls=%fused_computation.4 | convolution fusion | flops 2418376704 | bytes 13173504 | tf_op jit(solution)/shard_map/dot_general | solution.py:36
  87.4 255.0 %all-reduce.1 = bf16[768,2048]{1,0:T(8,128)(2,1)} all-reduce(f32[768,2048]{1,0:T(8,128)} %fusion.2), channel_id=1, replica_groups=mesh['dp'=64,'rep_0'=4,'rep_1'=2] {'rep_0','rep_1'}, use_global_device_ids=true, to_apply=%region_0.1 | all-reduce | flops 1572864 | bytes 9437184 | tf_op jit(solution)/shard_map/psum | solution.py:37
  342.4 0.0 reduce-scatter.2.cloned.1.call-done
  342.4 1.4 broadcast_multiply_fusion
  (1 shorter events, 0.0 us)
Async XLA Ops:
  7.2 70.7 %copy-start = (bf16[384,2048]{1,0:T(8,128)(2,1)S(1)}, bf16[384,2048]{1,0:T(8,128)(2,1)}, u32[]{:S(2)}) copy-start(bf16[384,2048]{1,0:T(8,128)(2,1)} %param.7) | copy-start | bytes 4718596
  7.2 65.0 %all-gather.2.cloned.1.call-start = ((), (), s32[]{:S(2)}) async-start(), calls=%async_computation.1 | async-start | bytes 3932160 | tf_op jit(solution)/shard_map/all_gather | solution.py:13
  20.4 322.0 %reduce-scatter.2.cloned.1.call-start = ((), (), s32[]{:S(2)}) async-start(), calls=%async_computation.2 | async-start | bytes 3194880 | tf_op jit(solution)/shard_map/reduce_scatter | solution.py:25
  77.8 1.4 copy-start.1
Sparse Core Ops, SparseCore 0:
  20.5 51.6 all-gather.1
  78.0 225.9 reduce-scatter.1
where the time goes:
time: 351 us
  blocking collectives  268 us (76%)
  waiting for transfers between devices  51.2 us (15%)
  between operations  14.7 us (4%)
  matrix products  13.7 us (4%)
    psum x1, blocking collectives, on_device(): input_sum = lax.psum(partial_terms, REP)  255 us
    all_gather x1, waiting for transfers between devices, whole_of(): nearer = lax.all_gather(array, axes[-1], axis=dim, tiled=True)  51.1 us
    all_gather x1, blocking collectives, whole_of(): nearer = lax.all_gather(array, axes[-1], axis=dim, tiled=True)  13.1 us
    dot_general x1, matrix products, on_device(): jnp.dot(pre_grad, up_weight, preferred_element_type=jnp.float32)  8.12 us
  transfers between devices with their start and end apart: 2, of which 1 were waited for; matrix products, arithmetic and copies ran while one was open for 2% of the time, Pallas kernels for 0%

commit v1 on v0

--- a/solution.py
+++ b/solution.py
@@ -34,7 +34,8 @@
     hidden_grad = jnp.dot(grad_live, down_weight, preferred_element_type=jnp.float32)
     pre_grad = jnp.where(pre_act > 0, hidden_grad, jnp.zeros_like(hidden_grad)).astype(jnp.bfloat16)
     partial_terms = jnp.dot(pre_grad, up_weight, preferred_element_type=jnp.float32)
-    input_sum = lax.psum(partial_terms, REP)
+    parts = lax.all_gather(partial_terms, REP)
+    input_sum = jnp.sum(parts, axis=0)
     input_grad = input_sum.astype(jnp.bfloat16)
     return (input_grad, down_grad)
 

time: 351 us -> 1290 us (3.68)
  the two profiles are of different devices: /device:TPU:4 before, /device:TPU:1 now
where the time goes in v1:
time: 1290 us
  waiting for transfers between devices  1220 us (95%)
  other arithmetic  21.1 us (2%)
  between operations  14.4 us (1%)
  matrix products  13.7 us (1%)
    all_gather x1, waiting for transfers between devices, on_device(): parts = lax.all_gather(partial_terms, REP)  971 us
    reduce_scatter x1, waiting for transfers between devices, on_device(): lax.psum_scatter(lax.dot_general(grad_live, hidden, (((0,), (0,)), ((), (...  198 us
    all_gather x1, waiting for transfers between devices, whole_of(): nearer = lax.all_gather(array, axes[-1], axis=dim, tiled=True)  55.1 us
  transfers between devices with their start and end apart: 3, of which 3 were waited for; matrix products, arithmetic and copies ran while one was open for 1% of the time, Pallas kernels for 0%

profile of v1, /device:TPU:1, one launch (start us, length us, event | category | flops | bytes accessed | tf_op | source)
XLA Modules:
  0.0 1285.2 jit_solution(15383877522979706606)
XLA Ops:
  7.2 0.0 copy-start
  7.2 0.0 all-gather.4.cloned.1.call-start
  7.2 10.0 all_gather.12
  17.3 0.0 all-gather.4.cloned.1.call-update
  17.3 0.0 reduce-scatter.2.cloned.1.call-start
  18.0 55.1 %all-gather.4.cloned.1.call-done = bf16[768,2048]{1,0:T(8,128)(2,1)} async-done(((bf16[768,512]{1,0:T(8,128)(2,1)}), bf16[768,2048]{1,0:T(8,128)(2,1)}) %all-gather.4.cloned.1.call-update) | async-done | bytes 3145744 | tf_op jit(solution)/shard_map/all_gather | solution.py:13
  73.1 5.7 fusion.1
  78.7 0.0 copy-start.2
  78.7 0.0 reduce-scatter.2.cloned.1.call-update
  78.7 0.0 all-gather.6.cloned.1.call-start
  78.8 0.0 copy-done
  78.8 1.3 copy-done.2
  80.1 8.1 fusion.2
  88.2 0.0 all-gather.6.cloned.1.call-update
  88.2 198.0 %reduce-scatter.2.cloned.1.call-done = f32[32,384]{1,0:T(8,128)} async-done(((f32[2048,384]{1,0:T(8,128)}), f32[32,384]{1,0:T(8,128)}) %reduce-scatter.2.cloned.1.call-update) | async-done | bytes 49168 | tf_op jit(solution)/shard_map/reduce_scatter | solution.py:25
  286.2 1.4 broadcast_multiply_fusion
  287.6 971.4 %all-gather.6.cloned.1.call-done = f32[6144,2048]{1,0:T(8,128)} async-done(((f32[768,2048]{1,0:T(8,128)}), f32[6144,2048]{1,0:T(8,128)}) %all-gather.6.cloned.1.call-update) | async-done | bytes 50331664 | tf_op jit(solution)/shard_map/all_gather | solution.py:37
  1259.0 0.0 copy-start.1
  1259.0 19.7 %reduce_sum.9 = bf16[768,2048]{1,0:T(8,128)(2,1)} reduce(f32[8,768,2048]{2,1,0:T(8,128)} %bitcast.5, f32[]{:T(128)} %constant.4.clone.1), dimensions={0}, to_apply=%region_0.1 | reduce | flops 11010048 | bytes 53477380 | tf_op jit(solution)/shard_map/reduce_sum | solution.py:38
  1278.7 0.0 copy-done.1
  (1 shorter events, 0.0 us)
Async XLA Ops:
  7.2 71.6 %copy-start = (bf16[384,2048]{1,0:T(8,128)(2,1)S(1)}, bf16[384,2048]{1,0:T(8,128)(2,1)}, u32[]{:S(2)}) copy-start(bf16[384,2048]{1,0:T(8,128)(2,1)} %param.7) | copy-start | bytes 4718596
  7.2 65.9 %all-gather.4.cloned.1.call-start = ((), (), s32[]{:S(2)}) async-start(), calls=%async_computation.1 | async-start | bytes 3932160 | tf_op jit(solution)/shard_map/all_gather | solution.py:13
  17.3 268.9 %reduce-scatter.2.cloned.1.call-start = ((), (), s32[]{:S(2)}) async-start(), calls=%async_computation.2 | async-start | bytes 3194880 | tf_op jit(solution)/shard_map/reduce_scatter | solution.py:25
  78.7 1.4 copy-start.2
  78.7 1180.3 %all-gather.6.cloned.1.call-start = ((), (), s32[]{:S(2)}) async-start(), calls=%async_computation.3 | async-start | bytes 56623104 | tf_op jit(solution)/shard_map/all_gather | solution.py:37
  1259.0 19.7 %copy-start.1 = (bf16[384,2048]{1,0:T(8,128)(2,1)S(1)}, bf16[384,2048]{1,0:T(8,128)(2,1)}, u32[]{:S(2)}) copy-start(bf16[384,2048]{1,0:T(8,128)(2,1)} %param.7) | copy-start | bytes 4718596
Sparse Core Ops, SparseCore 0:
  17.4 55.6 all-gather.3
  78.9 207.2 reduce-scatter.1
  288.3 970.7 all-gather.5

commit v2 on v0

--- a/solution.py
+++ b/solution.py
@@ -34,7 +34,9 @@
     hidden_grad = jnp.dot(grad_live, down_weight, preferred_element_type=jnp.float32)
     pre_grad = jnp.where(pre_act > 0, hidden_grad, jnp.zeros_like(hidden_grad)).astype(jnp.bfloat16)
     partial_terms = jnp.dot(pre_grad, up_weight, preferred_element_type=jnp.float32)
-    input_sum = lax.psum(partial_terms, REP)
+    input_sum = partial_terms
+    for over in ("rep_1", "rep_0"):
+        input_sum = lax.psum(input_sum, over)
     input_grad = input_sum.astype(jnp.bfloat16)
     return (input_grad, down_grad)
 

time: 351 us -> 592 us (1.69)
  waiting for transfers between devices: 51.2 us -> 434 us
  blocking collectives: 268 us -> 127 us
    reduce_scatter x1, waiting for transfers between devices: 0.01 us -> 208 us  [on_device(): lax.psum_scatter(lax.dot_general(grad_live, hidden, (((0,), (0,)), ((), (...]
    psum x0 -> x1, waiting for transfers between devices: none -> 175 us  [on_device(): input_sum = lax.psum(input_sum, over)]
    psum x1, blocking collectives: 255 us -> 114 us  [on_device(): input_sum = lax.psum(input_sum, over)]
  transfers between devices with their start and end apart: 2 -> 3, of which waited for: 1 -> 3; matrix products, arithmetic and copies ran while one was open for 2% -> 2% of each run, Pallas kernels for 0% -> 0%
where the time goes in v2:
time: 592 us
  waiting for transfers between devices  434 us (73%)
  blocking collectives  127 us (21%)
  between operations  14.4 us (2%)
  matrix products  13.8 us (2%)
    reduce_scatter x1, waiting for transfers between devices, on_device(): lax.psum_scatter(lax.dot_general(grad_live, hidden, (((0,), (0,)), ((), (...  208 us
    psum x1, waiting for transfers between devices, on_device(): input_sum = lax.psum(input_sum, over)  175 us
    psum x1, blocking collectives, on_device(): input_sum = lax.psum(input_sum, over)  114 us
    all_gather x1, waiting for transfers between devices, whole_of(): nearer = lax.all_gather(array, axes[-1], axis=dim, tiled=True)  51.1 us
    all_gather x1, blocking collectives, whole_of(): nearer = lax.all_gather(array, axes[-1], axis=dim, tiled=True)  13.1 us
  transfers between devices with their start and end apart: 3, of which 3 were waited for; matrix products, arithmetic and copies ran while one was open for 2% of the time, Pallas kernels for 0%

profile of v2, /device:TPU:4, one launch (start us, length us, event | category | flops | bytes accessed | tf_op | source)
XLA Modules:
  0.0 592.0 jit_solution(7643836721390185781)
XLA Ops:
  7.2 0.0 copy-start
  7.2 0.0 all-gather.2.cloned.1.call-start
  7.2 13.1 %all_gather.6 = bf16[768,512]{1,0:T(8,128)(2,1)} all-gather(bf16[768,256]{1,0:T(8,128)(2,1)} %param.5), channel_id=1, replica_groups=mesh['dp'=64,'rep_0'=4,'rep_1'=2] {'rep_1'}, dimensions={1}, use_global_device_ids=true | all-gather | bytes 1179648 | tf_op jit(solution)/shard_map/all_gather | solution.py:13
  20.3 0.0 all-gather.2.cloned.1.call-update
  20.4 0.0 reduce-scatter.2.cloned.1.call-start
  21.1 51.1 %all-gather.2.cloned.1.call-done = bf16[768,2048]{1,0:T(8,128)(2,1)} async-done(((bf16[768,512]{1,0:T(8,128)(2,1)}), bf16[768,2048]{1,0:T(8,128)(2,1)}) %all-gather.2.cloned.1.call-update) | async-done | bytes 3145744 | tf_op jit(solution)/shard_map/all_gather | solution.py:13
  72.2 5.7 fusion.1
  77.9 0.0 copy-start.1
  77.9 0.0 reduce-scatter.2.cloned.1.call-update
  77.9 0.0 all-reduce.3.cloned.1.call-start
  77.9 0.0 copy-done
  77.9 1.3 copy-done.1
  79.3 8.1 %fusion.2 = f32[768,2048]{1,0:T(8,128)} fusion(bf16[384,2048]{1,0:T(8,128)(2,1)S(1)} %copy-done, bf16[2048,384]{1,0:T(8,128)(2,1)S(1)} %copy-done.1, bf16[768,2048]{1,0:T(8,128)(2,1)} %all-gather.2.cloned.1.call-done, pred[768]{0:T(1024)(128)(4,1)S(1)} %iota_compare_fusion, bf16[768,384]{1,0:T(8,128)(2,1)} %param.6), kind=kOutput, calls=%fused_computation.4 | convolution fusion | flops 2418376704 | bytes 13173504 | tf_op jit(solution)/shard_map/dot_general | solution.py:36
  87.4 0.0 all-reduce.3.cloned.1.call-update
  87.4 208.0 %reduce-scatter.2.cloned.1.call-done = f32[32,384]{1,0:T(8,128)} async-done(((f32[2048,384]{1,0:T(8,128)}), f32[32,384]{1,0:T(8,128)}) %reduce-scatter.2.cloned.1.call-update) | async-done | bytes 49168 | tf_op jit(solution)/shard_map/reduce_scatter | solution.py:25
  295.4 1.4 broadcast_multiply_fusion
  296.8 174.7 %all-reduce.3.cloned.1.call-done = f32[768,2048]{1,0:T(8,128)} async-done(((f32[768,2048]{1,0:T(8,128)}), f32[768,2048]{1,0:T(8,128)}) %all-reduce.3.cloned.1.call-update) | async-done | bytes 6291472 | tf_op jit(solution)/shard_map/psum | solution.py:39
  471.5 113.9 %all-reduce.4 = bf16[768,2048]{1,0:T(8,128)(2,1)} all-reduce(f32[768,2048]{1,0:T(8,128)} %all-reduce.3.cloned.1.call-done), channel_id=1, replica_groups=mesh['dp'=64,'rep_0'=4,'rep_1'=2] {'rep_0'}, use_global_device_ids=true, to_apply=%region_1.2 | all-reduce | flops 1572864 | bytes 9437184 | tf_op jit(solution)/shard_map/psum | solution.py:39
  (1 shorter events, 0.0 us)
Async XLA Ops:
  7.2 70.8 %copy-start = (bf16[384,2048]{1,0:T(8,128)(2,1)S(1)}, bf16[384,2048]{1,0:T(8,128)(2,1)}, u32[]{:S(2)}) copy-start(bf16[384,2048]{1,0:T(8,128)(2,1)} %param.7) | copy-start | bytes 4718596
  7.2 65.0 %all-gather.2.cloned.1.call-start = ((), (), s32[]{:S(2)}) async-start(), calls=%async_computation.1 | async-start | bytes 3932160 | tf_op jit(solution)/shard_map/all_gather | solution.py:13
  20.4 275.0 %reduce-scatter.2.cloned.1.call-start = ((), (), s32[]{:S(2)}) async-start(), calls=%async_computation.3 | async-start | bytes 3194880 | tf_op jit(solution)/shard_map/reduce_scatter | solution.py:25
  77.9 1.4 copy-start.1
  77.9 393.6 %all-reduce.3.cloned.1.call-start = ((), (), s32[]{:S(2)}) async-start(), calls=%async_computation.2 | async-start | bytes 12582912 | tf_op jit(solution)/shard_map/psum | solution.py:39
Sparse Core Ops, SparseCore 0:
  20.5 51.6 all-gather.1
  78.0 217.3 reduce-scatter.1
  298.4 173.0 all-reduce.2
